TPU v7x, 32 devices: a whole 2x2x4 slice. The times are simulated.
32 devices in a mesh: row: 8 (over y, x, core), col: 4 (over z).
Axes of the slice: x: 2, y: 2, z: 4, core: 2. Of those that a mesh axis runs over, the one named last changes fastest.
Arguments:
- sensitivity: bfloat16 [512, 24576], P(('row', 'col')), may hold values from -0.25 to 0.25
- sensor_of_row: int32 [512], P(('row', 'col')), may hold values from 0 to 127
- row_class: int32 [512], P(('row', 'col')), may hold values from 0 to 3
- sensor_precision: float32 [128], replicated, may hold values from 0.25 to 4
- class_weight: float32 [4], replicated, may hold values from 0.25 to 2.5
Outputs:
- hessian: float32 [4, 24576, 6144], P('col', 'row')
All inputs are finite; a program needn't handle non-finite values.
Results may differ from a plain program's by a relative error of at most 0.004.
Values may be sent and summed in bfloat16 or wider, within the bound.
A program may use at most 192 MiB of HBM per device.

v0:
```python
import jax
import jax.numpy as jnp
from jax import lax
from jax.sharding import PartitionSpec as P


def contract(left, right):
    return lax.dot_general(
        left, right, (((0,), (0,)), ((), ())), preferred_element_type=jnp.float32
    )


def shards(sensitivity, sensor_of_row, row_class, sensor_precision, class_weight):
    row_count = lax.axis_size("row")
    col_count = lax.axis_size("col")
    width = sensitivity.shape[1]
    tile_width = width // row_count
    piece_width = tile_width // col_count
    col_index = lax.axis_index("col")
    sensor_match = (
        sensor_of_row[:, None] == jnp.arange(sensor_precision.shape[0], dtype=jnp.int32)[None, :]
    )
    class_match = row_class[:, None] == jnp.arange(class_weight.shape[0], dtype=jnp.int32)[None, :]
    precision = jnp.sum(jnp.where(sensor_match, sensor_precision[None, :], 0.0), axis=1)
    quality = jnp.sum(jnp.where(class_match, class_weight[None, :], 0.0), axis=1)
    scaled = (jnp.sqrt(precision * quality)[:, None] * sensitivity.astype(jnp.float32)).astype(
        jnp.bfloat16
    )
    pieces = lax.all_to_all(scaled, ("row", "col"), split_axis=1, concat_axis=0, tiled=True)
    own_tile = lax.all_gather(pieces, "col", axis=1, tiled=True)
    my_piece = lax.dynamic_slice_in_dim(own_tile, col_index * piece_width, piece_width, 1)
    block = contract(own_tile, lax.all_gather(my_piece, "row", axis=1, tiled=True))
    return block[None]


def solution(mesh):
    return jax.shard_map(
        shards,
        mesh=mesh,
        in_specs=(P(("row", "col"), None), P(("row", "col")), P(("row", "col")), P(), P()),
        out_specs=P("col", "row", None),
        check_vma=False,
    )
```

profile of v0, /device:TPU:0, one launch (start us, length us, event | category | flops | bytes accessed | tf_op | source)
XLA Modules:
  0.0 187.6 jit_solution(11318577829438510996)
XLA Ops:
  6.5 0.0 all-gather.3.cloned.1.call-start
  6.5 0.9 select_reduce_fusion
  7.4 0.8 select_reduce_fusion.1
  8.2 1.3 multiply_convert_fusion
  9.5 0.1 copy.11
  9.6 26.8 %all_to_all.19 = bf16[16,32,768]{2,0,1:T(8,128)(2,1)} all-to-all(bf16[16,32,768]{2,0,1:T(8,128)(2,1)S(1)} %bitcast.13), channel_id=1, replica_groups=mesh['row'=8,'col'=4] {'row','col'}, dimensions={1} | all-to-all | bytes 1572864 | tf_op jit(solution)/shard_map/all_to_all | solution.py:29
  36.4 0.0 all-gather.3.cloned.1.call-update
  36.4 0.0 all-gather.5.cloned.1.call-start
  36.5 63.3 %all-gather.3.cloned.1.call-done = bf16[512,3072]{1,0:T(8,128)(2,1)} async-done(((bf16[512,768]{1,0:T(8,128)(2,1)}), bf16[512,3072]{1,0:T(8,128)(2,1)}) %all-gather.3.cloned.1.call-update) | async-done | bytes 3145744 | tf_op jit(solution)/shard_map/all_gather | solution.py:30
  99.8 2.1 %constant_dynamic-slice_fusion = bf16[512,768]{1,0:T(8,128)(2,1)} fusion(bf16[512,3072]{1,0:T(8,128)(2,1)} %all-gather.3.cloned.1.call-done, s32[]{:T(128)S(6)} %select_n.13), kind=kLoop, calls=%fused_computation.8 | loop fusion | bytes 1572868 | tf_op jit(solution)/shard_map/dynamic_slice | solution.py:31
  101.9 0.0 all-gather.5.cloned.1.call-update
  101.9 44.2 %all-gather.5.cloned.1.call-done = bf16[512,6144]{1,0:T(8,128)(2,1)} async-done(((bf16[512,768]{1,0:T(8,128)(2,1)}), bf16[512,6144]{1,0:T(8,128)(2,1)}) %all-gather.5.cloned.1.call-update) | async-done | bytes 6291472 | tf_op jit(solution)/shard_map/all_gather | solution.py:32
  146.1 34.6 %convolution_bitcast_fusion = f32[1,3072,6144]{2,1,0:T(8,128)} fusion(bf16[512,3072]{1,0:T(8,128)(2,1)} %all-gather.3.cloned.1.call-done, bf16[512,6144]{1,0:T(8,128)(2,1)} %all-gather.5.cloned.1.call-done), kind=kOutput, calls=%fused_computation | convolution fusion | flops 19327352832 | bytes 84934656 | tf_op jit(solution)/shard_map/dot_general | solution.py:8
  (1 shorter events, 0.0 us)
Async XLA Ops:
  6.5 93.3 %all-gather.3.cloned.1.call-start = ((), (), s32[]{:S(2)}) async-start(), calls=%async_computation.1 | async-start | bytes 3932160 | tf_op jit(solution)/shard_map/all_gather | solution.py:30
  36.4 109.7 %all-gather.5.cloned.1.call-start = ((), (), s32[]{:S(2)}) async-start(), calls=%async_computation.2 | async-start | bytes 7077888 | tf_op jit(solution)/shard_map/all_gather | solution.py:32
Sparse Core Ops, SparseCore 0:
  36.5 63.2 all-gather.2
  102.0 44.0 all-gather.4
where the time goes:
time: 188 us
  waiting for transfers between devices  108 us (57%)
  matrix products  34.6 us (18%)
  blocking collectives  26.8 us (14%)
  between operations  13.4 us (7%)
  other arithmetic  2.95 us (2%)
  local copies, waits for them, and re-layouts  2.11 us (1%)
    all_gather x1, waiting for transfers between devices, shards(): own_tile = lax.all_gather(pieces, 'col', axis=1, tiled=True)  63.3 us
    all_gather x1, waiting for transfers between devices, shards(): lax.all_gather(my_piece, 'row', axis=1, tiled=True)  44.2 us
    dot_general x1, matrix products, contract(): lax.dot_general(left, right, (((0,), (0,)), ((), ())), preferred_element_...  34.6 us
    all_to_all x1, blocking collectives, shards(): lax.all_to_all(scaled, ('row', 'col'), split_axis=1, concat_axis=0, tiled...  26.8 us
  transfers between devices with their start and end apart: 2, of which 2 were waited for; matrix products, arithmetic and copies ran while one was open for 0% of the time, Pallas kernels for 0%

commit v1 on v0

--- a/solution.py
+++ b/solution.py
@@ -2,6 +2,12 @@
 import jax.numpy as jnp
 from jax import lax
 from jax.sharding import PartitionSpec as P
+
+
+def trade_parts(array, axis, split, join):
+    parts = jnp.split(array, lax.axis_size(axis), axis=split)
+    incoming = lax.all_to_all(jnp.stack(parts), axis, 0, 0)
+    return jnp.concatenate(incoming, axis=join)
 
 
 def contract(left, right):
@@ -26,7 +32,7 @@
     scaled = (jnp.sqrt(precision * quality)[:, None] * sensitivity.astype(jnp.float32)).astype(
         jnp.bfloat16
     )
-    pieces = lax.all_to_all(scaled, ("row", "col"), split_axis=1, concat_axis=0, tiled=True)
+    pieces = trade_parts(scaled, ("row", "col"), 1, 0)
     own_tile = lax.all_gather(pieces, "col", axis=1, tiled=True)
     my_piece = lax.dynamic_slice_in_dim(own_tile, col_index * piece_width, piece_width, 1)
     block = contract(own_tile, lax.all_gather(my_piece, "row", axis=1, tiled=True))

time: 188 us -> 188 us (level)
  no operation moved by 1% of the time
where the time goes in v1:
time: 188 us
  waiting for transfers between devices  108 us (57%)
  matrix products  34.7 us (18%)
  blocking collectives  26.8 us (14%)
  between operations  13.7 us (7%)
  other arithmetic  2.95 us (2%)
  local copies, waits for them, and re-layouts  2.2 us (1%)
    all_gather x1, waiting for transfers between devices, shards(): own_tile = lax.all_gather(pieces, 'col', axis=1, tiled=True)  63.3 us
    all_gather x1, waiting for transfers between devices, shards(): lax.all_gather(my_piece, 'row', axis=1, tiled=True)  44.2 us
    dot_general x1, matrix products, contract(): lax.dot_general(left, right, (((0,), (0,)), ((), ())), preferred_element_...  34.7 us
    all_to_all x1, blocking collectives, trade_parts(): incoming = lax.all_to_all(jnp.stack(parts), axis, 0, 0)  26.8 us
  transfers between devices with their start and end apart: 2, of which 2 were waited for; matrix products, arithmetic and copies ran while one was open for 0% of the time, Pallas kernels for 0%

profile of v1, /device:TPU:0, one launch (start us, length us, event | category | flops | bytes accessed | tf_op | source)
XLA Modules:
  0.0 187.9 jit_solution(5868822057229475340)
XLA Ops:
  6.5 0.0 all-gather.3.cloned.1.call-start
  6.5 0.9 select_reduce_fusion
  7.4 0.8 select_reduce_fusion.1
  8.2 1.3 multiply_convert_fusion
  9.9 26.8 %all_to_all.5 = bf16[32,16,768]{2,1,0:T(8,128)(2,1)} all-to-all(bf16[32,16,768]{2,1,0:T(8,128)(2,1)S(1)} %constant_dynamic-update-slice_fusion), channel_id=1, replica_groups=mesh['row'=8,'col'=4] {'row','col'}, dimensions={0} | all-to-all | bytes 1572864 | tf_op jit(solution)/shard_map/all_to_all | solution.py:9
  36.7 0.0 all-gather.3.cloned.1.call-update
  36.7 0.0 all-gather.5.cloned.1.call-start
  36.8 63.3 %all-gather.3.cloned.1.call-done = bf16[512,3072]{1,0:T(8,128)(2,1)} async-done(((bf16[512,768]{1,0:T(8,128)(2,1)}), bf16[512,3072]{1,0:T(8,128)(2,1)}) %all-gather.3.cloned.1.call-update) | async-done | bytes 3145744 | tf_op jit(solution)/shard_map/all_gather | solution.py:36
  100.1 2.1 %constant_dynamic-slice_fusion = bf16[512,768]{1,0:T(8,128)(2,1)} fusion(bf16[512,3072]{1,0:T(8,128)(2,1)} %all-gather.3.cloned.1.call-done, s32[]{:T(128)S(6)} %select_n.13), kind=kLoop, calls=%fused_computation.71 | loop fusion | bytes 1572868 | tf_op jit(solution)/shard_map/dynamic_slice | solution.py:37
  102.2 0.0 all-gather.5.cloned.1.call-update
  102.2 44.2 %all-gather.5.cloned.1.call-done = bf16[512,6144]{1,0:T(8,128)(2,1)} async-done(((bf16[512,768]{1,0:T(8,128)(2,1)}), bf16[512,6144]{1,0:T(8,128)(2,1)}) %all-gather.5.cloned.1.call-update) | async-done | bytes 6291472 | tf_op jit(solution)/shard_map/all_gather | solution.py:38
  146.4 34.7 %convolution_bitcast_fusion = f32[1,3072,6144]{2,1,0:T(8,128)} fusion(bf16[512,3072]{1,0:T(8,128)(2,1)} %all-gather.3.cloned.1.call-done, bf16[512,6144]{1,0:T(8,128)(2,1)} %all-gather.5.cloned.1.call-done), kind=kOutput, calls=%fused_computation | convolution fusion | flops 19327352832 | bytes 84934656 | tf_op jit(solution)/shard_map/dot_general | solution.py:14
  (33 shorter events, 0.1 us)
Async XLA Ops:
  6.5 93.6 %all-gather.3.cloned.1.call-start = ((), (), s32[]{:S(2)}) async-start(), calls=%async_computation.1 | async-start | bytes 3932160 | tf_op jit(solution)/shard_map/all_gather | solution.py:36
  36.7 109.7 %all-gather.5.cloned.1.call-start = ((), (), s32[]{:S(2)}) async-start(), calls=%async_computation.2 | async-start | bytes 7077888 | tf_op jit(solution)/shard_map/all_gather | solution.py:38
Sparse Core Ops, SparseCore 0:
  36.9 63.2 all-gather.2
  102.3 44.0 all-gather.4
